TPU v7x, 32 devices: a whole 2x2x4 slice. The times are simulated.
32 devices in a mesh: group: 2 (over y), dp: 4 (over x, core), tensor: 4 (over z).
Axes of the slice: x: 2, y: 2, z: 4, core: 2. Of those that a mesh axis runs over, the one named last changes fastest.
Arguments:
- x_feats: bfloat16 [4, 256, 8192], P(None, ('group', 'dp'), 'tensor'), parts along dimension 1, may hold values from -21 to 21, as said below
- w_query: bfloat16 [8192, 512], P(None, 'tensor'), may hold values from -0.0625 to 0.0625
- adapter_down: bfloat16 [64, 8192, 64], P(('group', 'dp'), 'tensor'), parts along dimension 0, may hold values from -0.0625 to 0.0625
- adapter_up: bfloat16 [64, 64, 512], P(('group', 'dp'), None, 'tensor'), parts along dimension 0, may hold values from -0.75 to 0.75
- agent_id: int32 [256], P(('group', 'dp')), parts along dimension 0, may hold values from 0 to 31, as said below
- adapter_slot: int32 [64], P('group'), parts along dimension 0, may hold values from 0 to 31, as said below
- cache_keys: bfloat16 [256, 192, 512], P(('group', 'dp', 'tensor')), parts along dimension 0, may hold values from -14 to 14, as said below
- cache_values: bfloat16 [256, 192, 512], P(('group', 'dp', 'tensor')), parts along dimension 0, may hold values from -6 to 6
- new_keys: bfloat16 [4, 256, 512], P(None, ('group', 'dp', 'tensor')), parts along dimension 1, may hold values from -6 to 6
- new_values: bfloat16 [4, 256, 512], P(None, ('group', 'dp', 'tensor')), parts along dimension 1, may hold values from -6 to 6
- lengths: int32 [256], P(('group', 'dp', 'tensor')), parts along dimension 0, may hold values from 1 to 192, as said below
Outputs:
- attended: bfloat16 [4, 256, 512], P(None, ('group', 'dp', 'tensor')), parts along dimension 1
There are 2 independent parts, one for each index of `group`. A program takes and returns all parts, laid end to end along the dimension named above; an argument that names none is the same for every part. Nothing has to cross between parts.
Inputs may be any that keep to these rules, and one draw needn't show every extreme that they name: `x_feats`: a draw of bounded magnitude. `cache_keys`: a draw of bounded magnitude. A permutation; the adapter of persona a is stored on dp index adapter_slot[a] // 8. `agent_id`: among the rows of one dp index at most 8 have adapters stored on any one dp index; in every draw one dp index stores the adapters of exactly 8 rows of every dp index. `lengths`: every device's rows include one of length 192.
All inputs are finite; a program needn't handle non-finite values.
Results may differ from a plain program's by a relative error of at most 0.009.
The roundings to bfloat16 on the way count: a program that leaves them out, or rounds other values in their place, can miss the bound.
Values may be sent and summed in bfloat16 or wider, within the bound.
A program may use at most 128 MiB of HBM per device.

v0:
```python
import jax
import jax.numpy as jnp
from jax import lax
from jax.sharding import PartitionSpec as P

HD = 128
KVH = 4


def attention(queries, key_cache, value_cache, fresh_keys, fresh_values, lengths):
    step_count, row_count, width = queries.shape
    group_size = width // (KVH * HD)
    length_max = key_cache.shape[1]
    score_scale = HD ** (-0.5)
    query_five = queries.reshape(step_count, row_count, KVH, group_size, HD)
    keys_four = key_cache.reshape(row_count, length_max, KVH, HD)
    values_four = value_cache.reshape(row_count, length_max, KVH, HD)
    fresh_four = fresh_keys.reshape(step_count, row_count, KVH, HD)
    fresh_vals = fresh_values.reshape(step_count, row_count, KVH, HD)
    old_scores = (
        jnp.einsum("srgqd,rjgd->srgqj", query_five, keys_four, preferred_element_type=jnp.float32)
        * score_scale
    )
    new_scores = (
        jnp.einsum("srgqd,trgd->srgqt", query_five, fresh_four, preferred_element_type=jnp.float32)
        * score_scale
    )
    valid_old = (jnp.arange(length_max)[None, :] < lengths[:, None])[None, :, None, None, :]
    valid_new = (jnp.arange(step_count)[None, :] <= jnp.arange(step_count)[:, None])[
        :, None, None, None, :
    ]
    scores = jnp.concatenate(
        [jnp.where(valid_old, old_scores, -jnp.inf), jnp.where(valid_new, new_scores, -jnp.inf)],
        axis=-1,
    )
    weights = jax.nn.softmax(scores, axis=-1).astype(jnp.bfloat16)
    mixed = jnp.einsum(
        "srgqj,rjgd->srgqd",
        weights[..., :length_max],
        values_four,
        preferred_element_type=jnp.float32,
    )
    mixed = mixed + jnp.einsum(
        "srgqt,trgd->srgqd",
        weights[..., length_max:],
        fresh_vals,
        preferred_element_type=jnp.float32,
    )
    return mixed.astype(jnp.bfloat16).reshape(step_count, row_count, width)


def local(
    x_feats,
    w_query,
    adapter_down,
    adapter_up,
    agent_id,
    adapter_slot,
    cache_keys,
    cache_values,
    new_keys,
    new_values,
    lengths,
):
    step_count, dp_rows, part_width = x_feats.shape
    width_q = w_query.shape[1]
    flat_feats = x_feats.reshape(step_count * dp_rows, part_width)
    base = jnp.dot(
        lax.all_gather(flat_feats, "tensor", axis=1, tiled=True),
        w_query,
        preferred_element_type=jnp.float32,
    )
    base = base.reshape(step_count, dp_rows, width_q)
    agent_count = adapter_slot.shape[0]
    match_agent = agent_id[:, None] == jnp.arange(agent_count, dtype=jnp.int32)[None, :]
    slot_ids = jnp.sum(jnp.where(match_agent, adapter_slot[None, :], 0), axis=1)
    n_dp = lax.axis_size("dp")
    ag_dev = adapter_down.shape[0]
    capacity = dp_rows // 4
    home_dev = slot_ids // ag_dev
    local_index = slot_ids % ag_dev
    at_home = (home_dev[:, None] == jnp.arange(n_dp, dtype=jnp.int32)[None, :]).astype(jnp.int32)
    place_in = jnp.sum((jnp.cumsum(at_home, axis=0) - 1) * at_home, axis=1)
    target = home_dev * capacity + place_in
    match_slot = jnp.arange(n_dp * capacity, dtype=jnp.int32)[:, None] == target[None, :]
    dispatch = match_slot.astype(jnp.bfloat16)
    outgoing = jnp.einsum("mr,srd->msd", dispatch, x_feats, preferred_element_type=jnp.float32)
    outgoing = outgoing.astype(jnp.bfloat16).reshape(n_dp, capacity, step_count, part_width)
    outgoing_index = jnp.sum(jnp.where(match_slot, local_index[None, :], 0), axis=1)
    outgoing_index = outgoing_index.reshape(n_dp, capacity)
    feats_in = lax.all_to_all(outgoing, "dp", split_axis=0, concat_axis=0, tiled=True)
    index_in = lax.all_to_all(outgoing_index, "dp", split_axis=0, concat_axis=0, tiled=True)
    items = feats_in.shape[1]
    flat_index = index_in.reshape(-1)
    chosen_down = adapter_down[flat_index]
    partial_low = jnp.einsum(
        "msd,mdk->msk",
        feats_in.reshape(-1, step_count, part_width),
        chosen_down,
        preferred_element_type=jnp.float32,
    )
    low_rank = lax.psum(partial_low, "tensor").astype(jnp.bfloat16)
    chosen_up = adapter_up[flat_index]
    correction = jnp.einsum("msk,mkq->msq", low_rank, chosen_up, preferred_element_type=jnp.float32)
    correction = correction.astype(jnp.bfloat16).reshape(n_dp, items, step_count, width_q)
    returned = lax.all_to_all(correction, "dp", split_axis=0, concat_axis=0, tiled=True)
    returned = returned.reshape(n_dp * capacity, step_count, width_q)
    delta_rows = jnp.einsum("mr,msq->srq", dispatch, returned, preferred_element_type=jnp.float32)
    queries = (base + delta_rows).astype(jnp.bfloat16)
    row_queries = lax.all_to_all(queries, "tensor", split_axis=1, concat_axis=2, tiled=True)
    return attention(row_queries, cache_keys, cache_values, new_keys, new_values, lengths)


def solution(mesh):
    return jax.shard_map(
        local,
        mesh=mesh,
        in_specs=(
            P(None, ("group", "dp"), "tensor"),
            P(None, "tensor"),
            P(("group", "dp"), "tensor", None),
            P(("group", "dp"), None, "tensor"),
            P(("group", "dp")),
            P("group"),
            P(("group", "dp", "tensor"), None, None),
            P(("group", "dp", "tensor"), None, None),
            P(None, ("group", "dp", "tensor"), None),
            P(None, ("group", "dp", "tensor"), None),
            P(("group", "dp", "tensor")),
        ),
        out_specs=P(None, ("group", "dp", "tensor"), None),
        check_vma=False,
    )
```

profile of v0, /device:TPU:0, one launch (start us, length us, event | category | flops | bytes accessed | tf_op | source)
XLA Modules:
  0.0 87.2 jit_solution(17017702036933388810)
XLA Ops:
  6.5 0.7 all-gather.2.cloned.1.call-update
  7.3 0.8 select_reduce_fusion.2
  8.5 0.7 all_to_all.24
  9.1 4.2 %all-to-all-start.1 = ((s32[4,1,8]{2,1,0:T(1,128)}), s32[4,1,8]{2,1,0:T(1,128)S(1)}, u32[]{:S(2)}, u32[]{:S(2)}) async-start(s32[4,1,8]{2,1,0:T(1,128)} %bitcast.5), calls=%async_computation.1 | async-start | bytes 4096 | tf_op jit(solution)/shard_map/all_to_all | solution.py:92
  13.3 1.5 %fusion = bf16[4,8,4,2048]{3,1,0,2:T(8,128)(2,1)S(1)} fusion(bf16[4,32,2048]{2,1,0:T(8,128)(2,1)} %param.11, s32[32]{0:T(128)S(1)} %multiply_add_fusion), kind=kOutput, calls=%fused_computation.3 | convolution fusion | flops 17040384 | bytes 1048704 | tf_op jit(solution)/shard_map/mr,srd->msd/dot_general | solution.py:87
  14.8 0.9 copy.39
  15.7 1.4 %all-to-all-done.1 = s32[4,1,8]{2,1,0:T(1,128)S(1)} async-done(((s32[4,1,8]{2,1,0:T(1,128)}), s32[4,1,8]{2,1,0:T(1,128)S(1)}, u32[]{:S(2)}, u32[]{:S(2)}) %all-to-all-start.1) | async-done | bytes 160 | tf_op jit(solution)/shard_map/all_to_all | solution.py:92
  17.0 3.5 %all-to-all-start = ((bf16[4,8,4,2048]{3,1,2,0:T(8,128)(2,1)}), bf16[4,8,4,2048]{3,1,2,0:T(8,128)(2,1)S(1)}, u32[]{:S(2)}, u32[]{:S(2)}) async-start(bf16[4,8,4,2048]{3,1,2,0:T(8,128)(2,1)} %copy.39), calls=%async_computation | async-start | bytes 1048576 | tf_op jit(solution)/shard_map/all_to_all | solution.py:91
  21.1 0.7 reduce.8
  21.9 5.0 %gather_fusion = bf16[32,2048,64]{1,2,0:T(8,128)(2,1)} fusion(bf16[8,2048,64]{1,2,0:T(8,128)(2,1)S(1)} %copy-done, s32[1024]{0:T(1024)S(1)} %pad_clamp_fusion), kind=kCustom, calls=%fused_computation | custom fusion | bytes 16777344 | tf_op jit(solution)/shard_map/gather | solution.py:95
  26.9 0.6 gather_fusion.1
  27.5 1.8 %all-to-all-done = bf16[4,8,4,2048]{3,1,2,0:T(8,128)(2,1)S(1)} async-done(((bf16[4,8,4,2048]{3,1,2,0:T(8,128)(2,1)}), bf16[4,8,4,2048]{3,1,2,0:T(8,128)(2,1)S(1)}, u32[]{:S(2)}, u32[]{:S(2)}) %all-to-all-start) | async-done | bytes 524320 | tf_op jit(solution)/shard_map/all_to_all | solution.py:91
  29.7 5.7 %fusion.54 = f32[32,4,64]{2,1,0:T(4,128)S(1)} fusion(bf16[32,4,2048]{2,1,0:T(4,128)(2,1)S(1)} %bitcast.105, bf16[32,2048,64]{1,2,0:T(8,128)(2,1)} %gather_fusion), kind=kOutput, calls=%fused_computation.65 | convolution fusion | flops 33554432 | bytes 8945664 | tf_op jit(solution)/shard_map/msd,mdk->msk/dot_general | solution.py:96
  35.4 22.5 %psum.7 = bf16[32,4,64]{2,1,0:T(4,128)(2,1)S(1)} all-reduce(f32[32,4,64]{2,1,0:T(4,128)S(1)} %fusion.54), channel_id=1, replica_groups=mesh['group'=2,'dp'=4,'tensor'=4] {'tensor'}, use_global_device_ids=true, to_apply=%region_4.5 | all-reduce | flops 8192 | bytes 49152 | tf_op jit(solution)/shard_map/psum | solution.py:102
  57.9 0.9 convolution_convert_fusion.1
  58.8 3.3 %all-to-all-start.2 = ((bf16[4,8,4,128]{3,2,1,0:T(4,128)(2,1)}), bf16[4,8,4,128]{3,2,1,0:T(4,128)(2,1)S(1)}, u32[]{:S(2)}, u32[]{:S(2)}) async-start(bf16[4,8,4,128]{3,2,1,0:T(4,128)(2,1)} %bitcast.7), calls=%async_computation.2 | async-start | bytes 65536 | tf_op jit(solution)/shard_map/all_to_all | solution.py:106
  62.1 2.9 %fusion.53 = f32[128,128]{1,0:T(8,128)S(1)} fusion(bf16[128,8192]{1,0:T(8,128)(2,1)} %all-gather.2.cloned.1.call-done, bf16[8192,128]{1,0:T(8,128)(2,1)} %param.12), kind=kOutput, calls=%fused_computation.64 | convolution fusion | flops 268435456 | bytes 4259840 | tf_op jit(solution)/shard_map/dot_general | solution.py:68
  65.0 0.9 %all-to-all-done.2 = bf16[4,8,4,128]{3,2,1,0:T(4,128)(2,1)S(1)} async-done(((bf16[4,8,4,128]{3,2,1,0:T(4,128)(2,1)}), bf16[4,8,4,128]{3,2,1,0:T(4,128)(2,1)S(1)}, u32[]{:S(2)}, u32[]{:S(2)}) %all-to-all-start.2) | async-done | bytes 32800 | tf_op jit(solution)/shard_map/all_to_all | solution.py:106
  66.1 0.6 copy.43
  66.8 3.3 %all-to-all-start.3 = ((bf16[4,32,128]{2,0,1:T(4,128)(2,1)}), bf16[4,32,128]{2,0,1:T(4,128)(2,1)S(1)}, u32[]{:S(2)}, u32[]{:S(2)}) async-start(bf16[4,32,128]{2,0,1:T(4,128)(2,1)} %copy.43), calls=%async_computation.3 | async-start | bytes 65536 | tf_op jit(solution)/shard_map/all_to_all | solution.py:110
  70.1 5.6 %all-to-all-done.3 = bf16[4,32,128]{2,0,1:T(4,128)(2,1)S(1)} async-done(((bf16[4,32,128]{2,0,1:T(4,128)(2,1)}), bf16[4,32,128]{2,0,1:T(4,128)(2,1)S(1)}, u32[]{:S(2)}, u32[]{:S(2)}) %all-to-all-start.3) | async-done | bytes 32800 | tf_op jit(solution)/shard_map/all_to_all | solution.py:110
  75.7 2.5 %fusion.51 = (f32[4,8,4]{0,2,1:T(4,128)S(1)}, f32[4,8,4,1,192]{4,0,2,1,3:T(4,128)S(1)}) fusion(bf16[4,4,8,128]{3,0,2,1:T(4,128)(2,1)S(1)} %bitcast.108, pred[8,192]{1,0:T(8,128)(4,1)S(1)} %iota_compare_fusion.3, bf16[8,192,512]{2,1,0:T(8,128)(2,1)} %param.17), kind=kOutput, calls=%fused_computation.62 | convolution fusion | flops 6365056 | bytes 1705984 | tf_op jit(solution)/shard_map/srgqd,rjgd->srgqj/dot_general | solution.py:21
  79.2 0.5 fusion.22
  79.7 0.6 copy.104
  (33 shorter events, 2.7 us)
Async XLA Ops:
  6.5 15.3 %copy-start = (bf16[8,2048,64]{1,2,0:T(8,128)(2,1)S(1)}, bf16[8,2048,64]{1,2,0:T(8,128)(2,1)}, u32[]{:S(2)}) copy-start(bf16[8,2048,64]{1,2,0:T(8,128)(2,1)} %param.13) | copy-start | bytes 6291460
  6.5 14.0 %copy-start.3 = (s32[8]{0:T(128)S(1)}, s32[8]{0:T(128)}, u32[]{:S(2)}) copy-start(s32[8]{0:T(128)} %param.21) | copy-start | bytes 100
  6.5 55.5 %all-gather.2.cloned.1.call-start = ((), (), s32[]{:S(2)}) async-start(), calls=%async_computation.4 | async-start | bytes 2621440 | tf_op jit(solution)/shard_map/all_gather | solution.py:69
  9.1 7.9 %all-to-all-start.1 = ((s32[4,1,8]{2,1,0:T(1,128)}), s32[4,1,8]{2,1,0:T(1,128)S(1)}, u32[]{:S(2)}, u32[]{:S(2)}) async-start(s32[4,1,8]{2,1,0:T(1,128)} %bitcast.5), calls=%async_computation.1 | async-start | bytes 4096 | tf_op jit(solution)/shard_map/all_to_all | solution.py:92
  17.0 12.3 %all-to-all-start = ((bf16[4,8,4,2048]{3,1,2,0:T(8,128)(2,1)}), bf16[4,8,4,2048]{3,1,2,0:T(8,128)(2,1)S(1)}, u32[]{:S(2)}, u32[]{:S(2)}) async-start(bf16[4,8,4,2048]{3,1,2,0:T(8,128)(2,1)} %copy.39), calls=%async_computation | async-start | bytes 1048576 | tf_op jit(solution)/shard_map/all_to_all | solution.py:91
  21.9 5.0 %copy-start.1 = (bf16[8,64,128]{2,1,0:T(8,128)(2,1)S(1)}, bf16[8,64,128]{2,1,0:T(8,128)(2,1)}, u32[]{:S(2)}) copy-start(bf16[8,64,128]{2,1,0:T(8,128)(2,1)} %param.14) | copy-start | bytes 393220
  58.8 7.2 %all-to-all-start.2 = ((bf16[4,8,4,128]{3,2,1,0:T(4,128)(2,1)}), bf16[4,8,4,128]{3,2,1,0:T(4,128)(2,1)S(1)}, u32[]{:S(2)}, u32[]{:S(2)}) async-start(bf16[4,8,4,128]{3,2,1,0:T(4,128)(2,1)} %bitcast.7), calls=%async_computation.2 | async-start | bytes 65536 | tf_op jit(solution)/shard_map/all_to_all | solution.py:106
  65.0 13.2 %copy-start.4 = (bf16[4,8,512]{2,1,0:T(8,128)(2,1)S(1)}, bf16[4,8,512]{2,1,0:T(8,128)(2,1)}, u32[]{:S(2)}) copy-start(bf16[4,8,512]{2,1,0:T(8,128)(2,1)} %param.19) | copy-start | bytes 98308
  65.0 13.9 %copy-start.5 = (bf16[4,8,512]{2,1,0:T(8,128)(2,1)S(1)}, bf16[4,8,512]{2,1,0:T(8,128)(2,1)}, u32[]{:S(2)}) copy-start(bf16[4,8,512]{2,1,0:T(8,128)(2,1)} %param.20) | copy-start | bytes 98308
  66.8 8.9 %all-to-all-start.3 = ((bf16[4,32,128]{2,0,1:T(4,128)(2,1)}), bf16[4,32,128]{2,0,1:T(4,128)(2,1)S(1)}, u32[]{:S(2)}, u32[]{:S(2)}) async-start(bf16[4,32,128]{2,0,1:T(4,128)(2,1)} %copy.43), calls=%async_computation.3 | async-start | bytes 65536 | tf_op jit(solution)/shard_map/all_to_all | solution.py:110
  75.7 3.5 %copy-start.2 = (bf16[8,192,512]{2,1,0:T(8,128)(2,1)S(1)}, bf16[8,192,512]{2,1,0:T(8,128)(2,1)}, u32[]{:S(2)}) copy-start(bf16[8,192,512]{2,1,0:T(8,128)(2,1)} %param.18) | copy-start | bytes 4718596
Sparse Core Ops, SparseCore 0:
  8.9 50.6 all-gather.1
where the time goes:
time: 87.7 us; the launch traced here: 87.2 us
  blocking collectives  22.5 us (26%)
  matrix products  14.7 us (17%)
  starting transfers between devices  14.2 us (16%)
  between operations  13.6 us (16%)
  waiting for transfers between devices  10.4 us (12%)
  local copies, waits for them, and re-layouts  9.49 us (11%)
  other arithmetic  2.4 us (3%)
    psum x1, blocking collectives, local(): low_rank = lax.psum(partial_low, 'tensor').astype(jnp.bfloat16)  22.5 us
    dot_general x1, matrix products, local(): jnp.einsum('msd,mdk->msk', feats_in.reshape(-1, step_count, part_width),...  5.7 us
    all_to_all x1, waiting for transfers between devices, local(): lax.all_to_all(queries, 'tensor', split_axis=1, concat_axis=2, tiled=True)  5.61 us
    gather x1, local copies, waits for them, and re-layouts, local(): chosen_down = adapter_down[flat_index]  5 us
    all_to_all x1, starting transfers between devices, local(): lax.all_to_all(outgoing_index, 'dp', split_axis=0, concat_axis=0, tiled=T...  4.21 us
    all_to_all x1, starting transfers between devices, local(): lax.all_to_all(outgoing, 'dp', split_axis=0, concat_axis=0, tiled=True)  3.48 us
    all_to_all x1, starting transfers between devices, local(): lax.all_to_all(queries, 'tensor', split_axis=1, concat_axis=2, tiled=True)  3.26 us
    all_to_all x1, starting transfers between devices, local(): lax.all_to_all(correction, 'dp', split_axis=0, concat_axis=0, tiled=True)  3.26 us
  transfers between devices with their start and end apart: 5, of which 4 were waited for; matrix products, arithmetic and copies ran while one was open for 23% of the time, Pallas kernels for 0%

commit v1 on v0

v1 whole, which is shorter than its diff:
```python
import functools

import jax
import jax.numpy as jnp
from jax import lax
from jax.experimental import pallas as pl
from jax.experimental.pallas import tpu as pltpu
from jax.sharding import PartitionSpec as P

HD = 128
KVH = 4
MESH = pl.DeviceIdType.MESH
LANES = 128
VMEM_BYTES = 60 * 1024 * 1024


def attention(queries, key_cache, value_cache, fresh_keys, fresh_values, lengths):
    step_count, row_count, width = queries.shape
    group_size = width // (KVH * HD)
    length_max = key_cache.shape[1]
    score_scale = HD ** (-0.5)
    query_five = queries.reshape(step_count, row_count, KVH, group_size, HD)
    keys_four = key_cache.reshape(row_count, length_max, KVH, HD)
    values_four = value_cache.reshape(row_count, length_max, KVH, HD)
    fresh_four = fresh_keys.reshape(step_count, row_count, KVH, HD)
    fresh_vals = fresh_values.reshape(step_count, row_count, KVH, HD)
    old_scores = (
        jnp.einsum("srgqd,rjgd->srgqj", query_five, keys_four, preferred_element_type=jnp.float32)
        * score_scale
    )
    new_scores = (
        jnp.einsum("srgqd,trgd->srgqt", query_five, fresh_four, preferred_element_type=jnp.float32)
        * score_scale
    )
    valid_old = (jnp.arange(length_max)[None, :] < lengths[:, None])[None, :, None, None, :]
    valid_new = (jnp.arange(step_count)[None, :] <= jnp.arange(step_count)[:, None])[
        :, None, None, None, :
    ]
    scores = jnp.concatenate(
        [jnp.where(valid_old, old_scores, -jnp.inf), jnp.where(valid_new, new_scores, -jnp.inf)],
        axis=-1,
    )
    weights = jax.nn.softmax(scores, axis=-1).astype(jnp.bfloat16)
    mixed = jnp.einsum(
        "srgqj,rjgd->srgqd",
        weights[..., :length_max],
        values_four,
        preferred_element_type=jnp.float32,
    )
    mixed = mixed + jnp.einsum(
        "srgqt,trgd->srgqd",
        weights[..., length_max:],
        fresh_vals,
        preferred_element_type=jnp.float32,
    )
    return mixed.astype(jnp.bfloat16).reshape(step_count, row_count, width)


def rows_of(index, size):
    return pl.ds(pl.multiple_of(index * size, size), size)


def queries_kernel(
    sizes,
    x_ref,
    w_ref,
    down_ref,
    up_ref,
    agent_row_ref,
    agent_col_ref,
    slot_row_ref,
    slot_col_ref,
    out_ref,
    w_parts,
    down_buf,
    x_out,
    x_in,
    low_out,
    low_in,
    low_all,
    corr_out,
    corr_in,
    delta_out,
    delta_in,
    base_out,
    base_in,
    copy_sem,
    z_send,
    z_recv,
    d_send,
    d_recv,
    b_send,
    b_recv,
    c_send,
    c_recv,
    l_send,
    l_recv,
    a_send,
    a_recv,
    r_send,
    r_recv,
    e_send,
    e_recv,
    s_send,
    s_recv,
):
    n_group, n_dp, n_tensor, steps, rows, capacity, adapters, rank = sizes
    depth = w_parts.shape[1]
    n_chip_x = n_dp // 2
    chips = n_group * n_chip_x
    piece = depth // (2 * chips)
    row_block = rows // n_tensor
    per_home = steps * capacity
    items = n_dp * per_home
    low_rows = items // n_tensor

    group = lax.axis_index("group")
    dp = lax.axis_index("dp")
    tensor = lax.axis_index("tensor")
    core = lax.rem(dp, 2)
    chip = group * n_chip_x + dp // 2

    def at_chip(number, which):
        return (number // n_chip_x, lax.rem(number, n_chip_x) * 2 + which, tensor)

    sibling = (group, (dp // 2) * 2 + (1 - core), tensor)

    def remote(src, dst, send, recv, device):
        return pltpu.make_async_remote_copy(
            src_ref=src, dst_ref=dst, send_sem=send, recv_sem=recv, device_id=device,
            device_id_type=MESH,
        )

    def up_t(k):
        return lax.rem(tensor + k, n_tensor)

    def from_t(k):
        return lax.rem(tensor - k + n_tensor, n_tensor)

    def up_d(j):
        return lax.rem(dp + j, n_dp)

    def from_d(j):
        return lax.rem(dp - j + n_dp, n_dp)

    own_w = pltpu.make_async_copy(w_ref.at[rows_of(tensor, depth)], w_parts.at[0], copy_sem.at[0])
    own_down = pltpu.make_async_copy(down_ref, down_buf, copy_sem.at[1])
    own_w.start()
    own_down.start()

    barrier = pltpu.get_barrier_semaphore()
    for k in range(1, n_tensor):
        pl.semaphore_signal(barrier, inc=1, device_id=(group, dp, up_t(k)), device_id_type=MESH)
    for j in range(1, n_dp):
        pl.semaphore_signal(barrier, inc=1, device_id=(group, up_d(j), tensor), device_id_type=MESH)
    for other in range(1, n_group):
        for j in range(n_dp):
            if j % 2 == 0:
                pl.semaphore_signal(
                    barrier, inc=1,
                    device_id=(lax.rem(group + other, n_group), up_d(j), tensor),
                    device_id_type=MESH,
                )
    pl.semaphore_wait(barrier, n_tensor - 1 + n_dp - 1 + (n_group - 1) * n_chip_x)

    mine = rows_of(chip * 2 + core, piece)

    def z_copy(k):
        start = up_t(k) * depth + (chip * 2 + core) * piece
        return remote(
            w_ref.at[pl.ds(pl.multiple_of(start, piece), piece)], w_parts.at[k, mine],
            z_send.at[k], z_recv.at[k], (group, dp, up_t(k)),
        )

    lax.fori_loop(1, n_tensor, lambda k, c: (z_copy(k).start(), c)[1], 0)

    agents = slot_row_ref.shape[1]
    width = steps * rows
    slot_lane = jnp.sum(
        jnp.where(
            lax.broadcasted_iota(jnp.int32, (agents, width), 0) == agent_row_ref[...],
            slot_col_ref[...], 0,
        ),
        axis=0, keepdims=True,
    )
    slot_sub = jnp.sum(
        jnp.where(
            lax.broadcasted_iota(jnp.int32, (rows, agents), 1) == agent_col_ref[...],
            slot_row_ref[...], 0,
        ),
        axis=1, keepdims=True,
    )
    home_lane = slot_lane // adapters
    home_sub = slot_sub // adapters
    row_lane = lax.rem(lax.broadcasted_iota(jnp.int32, (rows, width), 1), rows)
    earlier = (home_sub == home_lane) & (
        lax.broadcasted_iota(jnp.int32, (rows, width), 0) < row_lane
    )
    place_lane = jnp.sum(earlier.astype(jnp.int32), axis=0, keepdims=True)
    step_lane = lax.broadcasted_iota(jnp.int32, (1, width), 1) // rows
    target = jnp.where(
        place_lane < capacity, (home_lane * steps + step_lane) * capacity + place_lane, items
    )
    dispatch = jnp.where(
        lax.broadcasted_iota(jnp.int32, (items, width), 0) == target, 1.0, 0.0
    )
    local_index = jnp.sum(dispatch * (slot_lane - home_lane * adapters).astype(jnp.float32),
                          axis=1, keepdims=True)
    dispatch = dispatch.astype(jnp.bfloat16)
    sent = jnp.dot(dispatch, x_ref[...], preferred_element_type=jnp.float32)
    x_out[:, :, :depth] = sent.astype(jnp.bfloat16).reshape(n_dp, per_home, depth)
    x_out[:, :, depth:] = jnp.broadcast_to(local_index, (items, LANES)).astype(
        jnp.bfloat16
    ).reshape(n_dp, per_home, LANES)

    d_copies = []
    for j in range(1, n_dp):
        d_copies.append(
            remote(x_out.at[up_d(j)], x_in.at[dp], d_send.at[j], d_recv.at[j],
                   (group, up_d(j), tensor))
        )
        d_copies[-1].start()
    x_in[dp] = x_out[dp]

    def b_copy(k, q):
        return remote(
            w_parts.at[k, mine], w_parts.at[k, mine], b_send.at[k, q], b_recv.at[k, q],
            at_chip(lax.rem(chip + q, chips), core),
        )

    def c_copy(k, q):
        part = rows_of(lax.rem(chip - q + chips, chips) * 2 + core, piece)
        return remote(
            w_parts.at[k, part], w_parts.at[k, part], c_send.at[k, q], c_recv.at[k, q], sibling
        )

    def b_arrival(k, q):
        part = rows_of(lax.rem(chip - q + chips, chips) * 2 + core, piece)
        return remote(
            w_parts.at[k, part], w_parts.at[k, part], b_send.at[k, q], b_recv.at[k, q],
            at_chip(lax.rem(chip + q, chips), core),
        )

    def c_arrival(k, q):
        part = rows_of(lax.rem(chip - q + chips, chips) * 2 + 1 - core, piece)
        return remote(
            w_parts.at[k, part], w_parts.at[k, part], c_send.at[k, q], c_recv.at[k, q], sibling
        )

    def spread(k, carry):
        z_copy(k).wait_recv()
        for q in range(1, chips):
            b_copy(k, q).start()
        c_copy(k, 0).start()
        return carry

    def forward(k, carry):
        for q in range(1, chips):
            b_arrival(k, q).wait_recv()
            c_copy(k, q).start()
        return carry

    cut = [1 + (n_tensor - 1) * i // 3 for i in range(4)]
    lax.fori_loop(1, n_tensor, spread, 0)

    own_down.wait()
    for copy in d_copies:
        copy.wait_recv()
    arrived = x_in[...].reshape(items, depth + LANES)
    chosen = arrived[:, depth:].astype(jnp.float32)[:, :rank]
    dense = lax.dot_general(
        arrived[:, :depth], down_buf[...], (((1,), (1,)), ((), ())),
        preferred_element_type=jnp.float32,
    )
    low = jnp.zeros((items, rank), jnp.float32)
    for a in range(adapters):
        low += jnp.where(chosen == float(a), dense[:, a * rank:(a + 1) * rank], 0.0)
    low_out[...] = low.reshape(n_tensor, low_rows, rank)
    l_copies = []
    for k in range(1, n_tensor):
        l_copies.append(
            remote(low_out.at[up_t(k)], low_in.at[k], l_send.at[k], l_recv.at[k],
                   (group, dp, up_t(k)))
        )
        l_copies[-1].start()
    lax.fori_loop(cut[0], cut[1], forward, 0)
    total = low_out[tensor]
    for k in range(1, n_tensor):
        l_copies[k - 1].wait_recv()
        total += low_in[k]
    low_all[tensor] = total.astype(jnp.bfloat16)
    a_copies = []
    for k in range(1, n_tensor):
        a_copies.append(
            remote(low_all.at[tensor], low_all.at[tensor], a_send.at[k], a_recv.at[k],
                   (group, dp, up_t(k)))
        )
        a_copies[-1].start()
    lax.fori_loop(cut[1], cut[2], forward, 0)
    for k in range(1, n_tensor):
        remote(low_all.at[from_t(k)], low_all.at[from_t(k)], a_send.at[k], a_recv.at[k],
               (group, dp, up_t(k))).wait_recv()
    low_rank = low_all[...].reshape(items, rank).astype(jnp.float32)
    spread_low = jnp.concatenate(
        [jnp.where(chosen == float(a), low_rank, 0.0) for a in range(adapters)], axis=1
    ).astype(jnp.bfloat16)
    corr = jnp.dot(spread_low, up_ref[...], preferred_element_type=jnp.float32)
    corr_out[...] = corr.astype(jnp.bfloat16).reshape(corr_out.shape)
    r_copies = []
    for j in range(1, n_dp):
        r_copies.append(
            remote(corr_out.at[up_d(j)], corr_in.at[dp], r_send.at[j], r_recv.at[j],
                   (group, up_d(j), tensor))
        )
        r_copies[-1].start()
    corr_in[dp] = corr_out[dp]
    lax.fori_loop(cut[2], cut[3], forward, 0)

    def project(k):
        block = jnp.dot(x_ref[...], w_parts[k], preferred_element_type=jnp.float32)
        column = from_t(k)
        for t in range(n_tensor):
            for s in range(steps):
                base_out[t, column, s * row_block:(s + 1) * row_block, :] = block[
                    s * rows + t * row_block:s * rows + (t + 1) * row_block
                ]
        for j in range(1, n_tensor):
            remote(base_out.at[up_t(j), column], base_in.at[j, column], s_send.at[j],
                   s_recv.at[j], (group, dp, up_t(j))).start()

    own_w.wait()
    project(0)

    for copy in r_copies:
        copy.wait_recv()
    delta = lax.dot_general(
        dispatch, corr_in[...].reshape(items, corr_in.shape[2]), (((0,), (0,)), ((), ())),
        preferred_element_type=jnp.float32,
    )
    for t in range(n_tensor):
        delta_out[t] = jnp.concatenate(
            [delta[s * rows + t * row_block:s * rows + (t + 1) * row_block] for s in range(steps)],
            axis=0,
        ).astype(jnp.bfloat16)
    e_copies = []
    for k in range(1, n_tensor):
        e_copies.append(
            remote(delta_out.at[up_t(k)], delta_in.at[tensor], e_send.at[k], e_recv.at[k],
                   (group, dp, up_t(k)))
        )
        e_copies[-1].start()
    delta_in[tensor] = delta_out[tensor]

    def project_arrived(k, carry):
        for q in range(chips):
            c_arrival(k, q).wait_recv()
        project(k)
        return carry

    lax.fori_loop(1, n_tensor, project_arrived, 0)

    for copy in e_copies:
        copy.wait_recv()
    base = base_out[tensor]
    s_waits = []
    for j in range(1, n_tensor):
        s_waits.append(
            remote(base_out.at[up_t(j)], base_in.at[j], s_send.at[j], s_recv.at[j],
                   (group, dp, up_t(j)))
        )
        s_waits[-1].wait_recv()
        base += base_in[j]
    out_ref[...] = (base + delta_in[...].astype(jnp.float32)).astype(jnp.bfloat16)

    for copy in d_copies + l_copies + a_copies + r_copies + e_copies + s_waits:
        copy.wait_send()

    def drain(k, carry):
        z_copy(k).wait_send()
        for q in range(1, chips):
            b_copy(k, q).wait_send()
        for q in range(chips):
            c_copy(k, q).wait_send()
        return carry

    lax.fori_loop(1, n_tensor, drain, 0)


def local(
    x_feats,
    w_query,
    adapter_down,
    adapter_up,
    agent_id,
    adapter_slot,
    cache_keys,
    cache_values,
    new_keys,
    new_values,
    lengths,
):
    steps, rows, depth = x_feats.shape
    columns = w_query.shape[1]
    n_group, n_dp, n_tensor = (lax.axis_size(name) for name in ("group", "dp", "tensor"))
    adapters, _, rank = adapter_down.shape
    capacity = rows // 4
    row_block = rows // n_tensor
    per_home = steps * capacity
    items = n_dp * per_home
    chips = n_group * n_dp // 2
    sizes = (n_group, n_dp, n_tensor, steps, rows, capacity, adapters, rank)
    vmem = pl.BlockSpec(memory_space=pltpu.VMEM)
    hbm = pl.BlockSpec(memory_space=pl.ANY)
    bf16, f32 = jnp.bfloat16, jnp.float32
    own = steps * row_block
    dma = pltpu.SemaphoreType.DMA
    tensor_sems = [dma((n_tensor,)), dma((n_tensor,))]
    dp_sems = [dma((n_dp,)), dma((n_dp,))]
    queries = pl.pallas_call(
        functools.partial(queries_kernel, sizes),
        out_shape=jax.ShapeDtypeStruct((n_tensor, own, columns), bf16),
        in_specs=[vmem, hbm, hbm, vmem, vmem, vmem, vmem, vmem],
        out_specs=vmem,
        scratch_shapes=[
            pltpu.VMEM((n_tensor, depth, columns), bf16),
            pltpu.VMEM((adapters * rank, depth), bf16),
            pltpu.VMEM((n_dp, per_home, depth + LANES), bf16),
            pltpu.VMEM((n_dp, per_home, depth + LANES), bf16),
            pltpu.VMEM((n_tensor, items // n_tensor, rank), f32),
            pltpu.VMEM((n_tensor, items // n_tensor, rank), f32),
            pltpu.VMEM((n_tensor, items // n_tensor, rank), bf16),
            pltpu.VMEM((n_dp, per_home, columns), bf16),
            pltpu.VMEM((n_dp, per_home, columns), bf16),
            pltpu.VMEM((n_tensor, own, columns), bf16),
            pltpu.VMEM((n_tensor, own, columns), bf16),
            pltpu.VMEM((n_tensor, n_tensor, own, columns), f32),
            pltpu.VMEM((n_tensor, n_tensor, own, columns), f32),
            dma((2,)),
            *tensor_sems,
            *dp_sems,
            dma((n_tensor, chips)),
            dma((n_tensor, chips)),
            dma((n_tensor, chips)),
            dma((n_tensor, chips)),
            *tensor_sems,
            *tensor_sems,
            *dp_sems,
            *tensor_sems,
            *tensor_sems,
        ],
        compiler_params=pltpu.CompilerParams(
            collective_id=0, has_side_effects=True, vmem_limit_bytes=VMEM_BYTES
        ),
        name="queries",
    )(
        x_feats.reshape(steps * rows, depth),
        w_query,
        jnp.swapaxes(adapter_down, 1, 2).reshape(adapters * rank, depth),
        adapter_up.reshape(adapters * rank, columns),
        jnp.tile(agent_id, steps).reshape(1, steps * rows),
        agent_id.reshape(rows, 1),
        adapter_slot.reshape(1, -1),
        adapter_slot.reshape(-1, 1),
    )
    row_queries = queries.reshape(n_tensor, steps, row_block, columns)
    row_queries = row_queries.transpose(1, 2, 0, 3).reshape(steps, row_block, n_tensor * columns)
    return attention(row_queries, cache_keys, cache_values, new_keys, new_values, lengths)


def solution(mesh):
    return jax.shard_map(
        local,
        mesh=mesh,
        in_specs=(
            P(None, ("group", "dp"), "tensor"),
            P(None, "tensor"),
            P(("group", "dp"), "tensor", None),
            P(("group", "dp"), None, "tensor"),
            P(("group", "dp")),
            P("group"),
            P(("group", "dp", "tensor"), None, None),
            P(("group", "dp", "tensor"), None, None),
            P(None, ("group", "dp", "tensor"), None),
            P(None, ("group", "dp", "tensor"), None),
            P(("group", "dp", "tensor")),
        ),
        out_specs=P(None, ("group", "dp", "tensor"), None),
        check_vma=False,
    )
```

time: 87.7 us -> 44.1 us (0.50)
  Pallas kernels: 0 us -> 34.3 us
  blocking collectives: 22.5 us -> 0 us
  starting transfers between devices: 14.2 us -> 0 us
  between operations: 13.6 us -> 0.08 us
  matrix products: 14.7 us -> 3.61 us
  waiting for transfers between devices: 10.4 us -> 0 us
  local copies, waits for them, and re-layouts: 9.49 us -> 4.65 us
  other arithmetic: 2.4 us -> 1.31 us
    pallas_call x0 -> x1, Pallas kernels: none -> 34.3 us  [local(): pl.pallas_call(functools.partial(queries_kernel, sizes), out_shape=jax.Sh...]
    psum x1 -> x0, blocking collectives: 22.5 us -> none  [local(): low_rank = lax.psum(partial_low, 'tensor').astype(jnp.bfloat16)]
    all_to_all x4 -> x0, starting transfers between devices: 14.2 us -> none  [the longest x1 4.21 us: local(): lax.all_to_all(outgoing_index, 'dp', split_axis=0, concat_axis=0, tiled=T...]
    dot_general x5 -> x0, matrix products: 11.1 us -> none  [the longest x1 5.7 us: local(): jnp.einsum('msd,mdk->msk', feats_in.reshape(-1, step_count, part_width),...]
    all_to_all x4 -> x0, waiting for transfers between devices: 9.66 us -> none  [the longest x1 5.61 us: local(): lax.all_to_all(queries, 'tensor', split_axis=1, concat_axis=2, tiled=True)]
    gather x2 -> x0, local copies, waits for them, and re-layouts: 5.65 us -> none  [the longest x1 5 us: local(): chosen_down = adapter_down[flat_index]]
    reshape x2, local copies, waits for them, and re-layouts: 0.95 us -> 2.67 us  [the longest x1 1.34 us: local(): agent_id.reshape(rows, 1)]
    all_to_all x3 -> x0, local copies, waits for them, and re-layouts: 1.59 us -> none  [the longest x2 1.18 us: local(): lax.all_to_all(outgoing_index, 'dp', split_axis=0, concat_axis=0, tiled=T...]
  transfers between devices with their start and end apart: 5 -> 0, of which waited for: 4 -> 0; matrix products, arithmetic and copies ran while one was open for 23% -> 0% of each run, Pallas kernels for 0% -> 0%
where the time goes in v1:
time: 44.1 us; the launch traced here: 43.9 us
  Pallas kernels  34.3 us (78%)
  local copies, waits for them, and re-layouts  4.65 us (11%)
  matrix products  3.61 us (8%)
  other arithmetic  1.31 us (3%)
    pallas_call x1, Pallas kernels, local(): pl.pallas_call(functools.partial(queries_kernel, sizes), out_shape=jax.Sh...  34.3 us
    dot_general x1, matrix products, attention(): jnp.einsum('srgqd,rjgd->srgqj', query_five, keys_four, preferred_element_...  1.75 us
    reshape x1, local copies, waits for them, and re-layouts, local(): agent_id.reshape(rows, 1)  1.34 us
    reshape x1, local copies, waits for them, and re-layouts, local(): adapter_slot.reshape(-1, 1)  1.33 us
    another operation x2, local copies, waits for them, and re-layouts, local(): jnp.tile(agent_id, steps).reshape(1, steps * rows)  1.31 us
    dot_general x1, matrix products, attention(): jnp.einsum('srgqd,trgd->srgqt', query_five, fresh_four, preferred_element...  1.12 us

profile of v1, /device:TPU:0, one launch (start us, length us, event | category | flops | bytes accessed | tf_op | source)
XLA Modules:
  0.0 43.9 jit_solution(16411692628297760090)
XLA Ops:
  0.0 0.0 copy-start
  0.0 0.8 %iota_compare_fusion = pred[8,192]{1,0:T(8,128)(4,1)S(1)} fusion(s32[8]{0:T(128)} %param.21), kind=kLoop, calls=%fused_computation.30 | loop fusion | flops 1536 | bytes 1568 | tf_op jit(solution)/shard_map/lt | solution.py:35
  0.9 0.7 %tile.2 = s32[4,32]{1,0:T(4,128)S(1)} broadcast(s32[32]{0:T(128)} %param.15), dimensions={1} | broadcast | bytes 640 | tf_op jit(solution)/shard_map/tile | solution.py:460
  1.5 0.7 %reshape_tile.3.agent_row_ref = s32[1,128]{1,0:T(1,128)} reshape(s32[4,32]{1,0:T(4,128)S(1)} %tile.2) | data formatting | bytes 1024 | tf_op jit(solution)/shard_map/reshape;tile | solution.py:460
  2.2 1.3 %copy.20.slot_col_ref = s32[32,1]{1,0:T(8,128)} copy(s32[32,1]{0,1:T(1,128)} %bitcast.89) | data formatting | bytes 256 | tf_op jit(solution)/shard_map/reshape | solution.py:463
  3.5 1.3 %copy.19.agent_col_ref = s32[32,1]{1,0:T(8,128)} copy(s32[32,1]{0,1:T(1,128)} %bitcast.88) | data formatting | bytes 256 | tf_op jit(solution)/shard_map/reshape | solution.py:461
  4.8 0.0 copy-start.2
  4.8 34.3 %queries.1 = bf16[4,32,128]{2,1,0:T(8,128)(2,1)} custom-call(bf16[128,2048]{1,0:T(8,128)(2,1)} %bitcast.84, bf16[8192,128]{1,0:T(8,128)(2,1)} %w_ref.1, bf16[512,2048]{1,0:T(8,128)(2,1)} %bitcast.83, bf16[512,128]{1,0:T(8,128)(2,1)} %bitcast.85, s32[1,128]{1,0:T(1,128)} %reshape_tile.3.agent_row_ref, s32[32,1]{1,0:T(8,128)} %copy.19.agent_col_ref, ...), custom_call_target="tpu_custom_call" | custom-call | tf_op jit(solution)/shard_map/queries/pallas_call | solution.py:419
  39.1 0.0 copy-start.3
  39.1 0.0 copy-start.1
  39.1 0.0 copy-done.2
  39.1 1.1 %fusion.39 = (f32[4,8,4]{0,2,1:T(4,128)S(1)}, f32[4,8,4,1,4]{4,0,2,1,3:T(4,128)S(1)}) fusion(bf16[4,8,4,128]{3,1,2,0:T(8,128)(2,1)S(1)} %bitcast.91, bf16[4,4,8,128]{3,2,1,0:T(8,128)(2,1)} %bitcast.86, pred[4,4]{1,0:T(4,128)(4,1)S(1)} %iota_compare_fusion.1), kind=kOutput, calls=%fused_computation.33 | convolution fusion | flops 132480 | bytes 68112 | tf_op jit(solution)/shard_map/srgqd,trgd->srgqt/dot_general | solution.py:32
  40.3 0.0 copy-done
  40.3 1.8 %fusion.38 = (f32[4,8,4]{0,2,1:T(4,128)S(1)}, f32[4,8,4,1,192]{4,0,2,1,3:T(4,128)S(1)}) fusion(bf16[4,4,8,128]{3,2,1,0:T(8,128)(2,1)} %bitcast.87, pred[8,192]{1,0:T(8,128)(4,1)S(1)} %iota_compare_fusion, bf16[8,192,512]{2,1,0:T(8,128)(2,1)S(1)} %copy-done), kind=kOutput, calls=%fused_computation.32 | convolution fusion | flops 6365056 | bytes 1705984 | tf_op jit(solution)/shard_map/srgqd,rjgd->srgqj/dot_general | solution.py:28
  42.1 0.3 fusion.37
  42.3 0.2 divide_convert_fusion
  42.5 0.0 copy-done.3
  42.5 0.2 fusion.30
  42.7 0.0 copy-done.1
  42.8 0.5 %fusion.19 = bf16[4,8,4,1,128]{4,0,2,1,3:T(4,128)(2,1)S(1)} fusion(f32[8,4,4,128]{3,2,1,0:T(4,128)S(1)} %fusion.30, bf16[4,8,4,1,196]{4,0,2,1,3:T(4,128)(2,1)S(1)} %divide_convert_fusion, bf16[8,192,512]{2,1,0:T(8,128)(2,1)S(1)} %copy-done.1), kind=kOutput, calls=%fused_computation.12 | convolution fusion | flops 6324224 | bytes 1721344 | tf_op jit(solution)/shard_map/srgqj,rjgd->srgqd/dot_general | solution.py:44
  43.3 0.6 %copy.72 = bf16[4,8,4,1,128]{4,1,3,2,0:T(8,128)(2,1)} copy(bf16[4,8,4,1,128]{4,0,2,1,3:T(4,128)(2,1)S(1)} %fusion.19) | data formatting | bytes 65536 | tf_op jit(solution)/shard_map/convert_element_type | solution.py:56
  (2 shorter events, 0.0 us)
Async XLA Ops:
  0.0 40.3 %copy-start = (bf16[8,192,512]{2,1,0:T(8,128)(2,1)S(1)}, bf16[8,192,512]{2,1,0:T(8,128)(2,1)}, u32[]{:S(2)}) copy-start(bf16[8,192,512]{2,1,0:T(8,128)(2,1)} %param.17) | copy-start | bytes 4718596
  4.8 34.3 %copy-start.2 = (bf16[4,8,512]{2,1,0:T(8,128)(2,1)S(1)}, bf16[4,8,512]{2,1,0:T(8,128)(2,1)}, u32[]{:S(2)}) copy-start(bf16[4,8,512]{2,1,0:T(8,128)(2,1)} %param.19) | copy-start | bytes 98308
  39.1 3.4 %copy-start.3 = (bf16[4,8,512]{2,1,0:T(8,128)(2,1)S(1)}, bf16[4,8,512]{2,1,0:T(8,128)(2,1)}, u32[]{:S(2)}) copy-start(bf16[4,8,512]{2,1,0:T(8,128)(2,1)} %param.20) | copy-start | bytes 98308
  39.1 3.6 %copy-start.1 = (bf16[8,192,512]{2,1,0:T(8,128)(2,1)S(1)}, bf16[8,192,512]{2,1,0:T(8,128)(2,1)}, u32[]{:S(2)}) copy-start(bf16[8,192,512]{2,1,0:T(8,128)(2,1)} %param.18) | copy-start | bytes 4718596

commit v2 on v1

--- a/solution.py
+++ b/solution.py
@@ -14,62 +14,73 @@
 VMEM_BYTES = 60 * 1024 * 1024
 
 
-def attention(queries, key_cache, value_cache, fresh_keys, fresh_values, lengths):
-    step_count, row_count, width = queries.shape
-    group_size = width // (KVH * HD)
-    length_max = key_cache.shape[1]
-    score_scale = HD ** (-0.5)
-    query_five = queries.reshape(step_count, row_count, KVH, group_size, HD)
-    keys_four = key_cache.reshape(row_count, length_max, KVH, HD)
-    values_four = value_cache.reshape(row_count, length_max, KVH, HD)
-    fresh_four = fresh_keys.reshape(step_count, row_count, KVH, HD)
-    fresh_vals = fresh_values.reshape(step_count, row_count, KVH, HD)
-    old_scores = (
-        jnp.einsum("srgqd,rjgd->srgqj", query_five, keys_four, preferred_element_type=jnp.float32)
-        * score_scale
-    )
-    new_scores = (
-        jnp.einsum("srgqd,trgd->srgqt", query_five, fresh_four, preferred_element_type=jnp.float32)
-        * score_scale
-    )
-    valid_old = (jnp.arange(length_max)[None, :] < lengths[:, None])[None, :, None, None, :]
-    valid_new = (jnp.arange(step_count)[None, :] <= jnp.arange(step_count)[:, None])[
-        :, None, None, None, :
-    ]
-    scores = jnp.concatenate(
-        [jnp.where(valid_old, old_scores, -jnp.inf), jnp.where(valid_new, new_scores, -jnp.inf)],
-        axis=-1,
-    )
-    weights = jax.nn.softmax(scores, axis=-1).astype(jnp.bfloat16)
-    mixed = jnp.einsum(
-        "srgqj,rjgd->srgqd",
-        weights[..., :length_max],
-        values_four,
-        preferred_element_type=jnp.float32,
-    )
-    mixed = mixed + jnp.einsum(
-        "srgqt,trgd->srgqd",
-        weights[..., length_max:],
-        fresh_vals,
-        preferred_element_type=jnp.float32,
-    )
-    return mixed.astype(jnp.bfloat16).reshape(step_count, row_count, width)
+def attend(steps, row_block, parts, keys_buf, values_buf, fresh_keys, fresh_values, lengths, out_ref):
+    length_max = keys_buf.shape[1]
+    cached = row_block * length_max
+    queries = steps * row_block
+    per_part = parts[0].shape[1] // HD
+    group_size = len(parts) * per_part // KVH
+    total = group_size * queries
+    key_row = lax.broadcasted_iota(jnp.int32, (1, cached), 1) // length_max
+    key_at = lax.rem(lax.broadcasted_iota(jnp.int32, (1, cached), 1), length_max)
+    lane = lax.broadcasted_iota(jnp.int32, (1, row_block), 1)
+    limit = jnp.zeros((1, cached), jnp.int32)
+    for r in range(row_block):
+        one = jnp.sum(jnp.where(lane == r, lengths, 0), axis=1, keepdims=True)
+        limit = jnp.where(key_row == r, one, limit)
+    key_row = jnp.where(key_at < limit, key_row, -1)
+    query = lax.rem(lax.broadcasted_iota(jnp.int32, (total, 1), 0), queries)
+    query_row, query_step = lax.rem(query, row_block), query // row_block
+    old_valid = key_row == query_row
+    fresh = lax.broadcasted_iota(jnp.int32, (1, queries), 1)
+    new_valid = (lax.rem(fresh, row_block) == query_row) & (fresh // row_block <= query_step)
+    contract = (((1,), (1,)), ((), ()))
+    for g in range(KVH):
+        cols = slice(g * HD, (g + 1) * HD)
+        heads = range(g * group_size, (g + 1) * group_size)
+        q = [parts[h // per_part][:, (h % per_part) * HD:(h % per_part + 1) * HD] for h in heads]
+        q = (q[0] if len(q) == 1 else jnp.concatenate(q, axis=0)).astype(jnp.bfloat16)
+        keys = keys_buf[:, :, cols].reshape(cached, HD)
+        values = values_buf[:, :, cols].reshape(cached, HD)
+        old = lax.dot_general(q, keys, contract, preferred_element_type=jnp.float32)
+        new = lax.dot_general(
+            q, fresh_keys[:, cols], contract, preferred_element_type=jnp.float32
+        )
+        old = jnp.where(old_valid, old * HD ** (-0.5), -jnp.inf)
+        new = jnp.where(new_valid, new * HD ** (-0.5), -jnp.inf)
+        top = jnp.maximum(
+            jnp.max(old, axis=1, keepdims=True), jnp.max(new, axis=1, keepdims=True)
+        )
+        old, new = jnp.exp(old - top), jnp.exp(new - top)
+        norm = jnp.sum(old, axis=1, keepdims=True) + jnp.sum(new, axis=1, keepdims=True)
+        old, new = (old / norm).astype(jnp.bfloat16), (new / norm).astype(jnp.bfloat16)
+        mixed = jnp.dot(old, values, preferred_element_type=jnp.float32)
+        mixed += jnp.dot(new, fresh_values[:, cols], preferred_element_type=jnp.float32)
+        for i, h in enumerate(heads):
+            out_ref[:, :, h * HD:(h + 1) * HD] = (
+                mixed[i * queries:(i + 1) * queries]
+                .reshape(steps, row_block, HD)
+                .astype(jnp.bfloat16)
+            )
 
 
 def rows_of(index, size):
     return pl.ds(pl.multiple_of(index * size, size), size)
 
 
-def queries_kernel(
+def decode_kernel(
     sizes,
     x_ref,
     w_ref,
     down_ref,
     up_ref,
-    agent_row_ref,
-    agent_col_ref,
-    slot_row_ref,
-    slot_col_ref,
+    agent_ref,
+    slot_ref,
+    keys_ref,
+    values_ref,
+    new_keys_ref,
+    new_values_ref,
+    lengths_ref,
     out_ref,
     w_parts,
     down_buf,
@@ -84,6 +95,8 @@
     delta_in,
     base_out,
     base_in,
+    keys_buf,
+    values_buf,
     copy_sem,
     z_send,
     z_recv,
@@ -147,6 +160,8 @@
     own_down = pltpu.make_async_copy(down_ref, down_buf, copy_sem.at[1])
     own_w.start()
     own_down.start()
+    own_keys = pltpu.make_async_copy(keys_ref, keys_buf, copy_sem.at[2])
+    own_values = pltpu.make_async_copy(values_ref, values_buf, copy_sem.at[3])
 
     barrier = pltpu.get_barrier_semaphore()
     for k in range(1, n_tensor):
@@ -174,19 +189,29 @@
 
     lax.fori_loop(1, n_tensor, lambda k, c: (z_copy(k).start(), c)[1], 0)
 
-    agents = slot_row_ref.shape[1]
+    agents = slot_ref.shape[1]
     width = steps * rows
+
+    def as_column(row, count):
+        diagonal = lax.broadcasted_iota(jnp.int32, (count, count), 0) == lax.broadcasted_iota(
+            jnp.int32, (count, count), 1
+        )
+        return jnp.sum(jnp.where(diagonal, row, 0), axis=1, keepdims=True)
+
+    agent_row, slot_row = agent_ref[...], slot_ref[...]
+    agent_col, slot_col = as_column(agent_row, rows), as_column(slot_row, agents)
+    agent_row = jnp.concatenate([agent_row] * steps, axis=1)
     slot_lane = jnp.sum(
         jnp.where(
-            lax.broadcasted_iota(jnp.int32, (agents, width), 0) == agent_row_ref[...],
-            slot_col_ref[...], 0,
+            lax.broadcasted_iota(jnp.int32, (agents, width), 0) == agent_row,
+            slot_col, 0,
         ),
         axis=0, keepdims=True,
     )
     slot_sub = jnp.sum(
         jnp.where(
-            lax.broadcasted_iota(jnp.int32, (rows, agents), 1) == agent_col_ref[...],
-            slot_row_ref[...], 0,
+            lax.broadcasted_iota(jnp.int32, (rows, agents), 1) == agent_col,
+            slot_row, 0,
         ),
         axis=1, keepdims=True,
     )
@@ -261,6 +286,28 @@
         return carry
 
     cut = [1 + (n_tensor - 1) * i // 3 for i in range(4)]
+    def project(k):
+        block = jnp.dot(x_ref[...], w_parts[k], preferred_element_type=jnp.float32)
+        column = from_t(k)
+        for t in range(n_tensor):
+            for s in range(steps):
+                base_out[t, column, s * row_block:(s + 1) * row_block, :] = block[
+                    s * rows + t * row_block:s * rows + (t + 1) * row_block
+                ]
+        for j in range(1, n_tensor):
+            remote(base_out.at[up_t(j), column], base_in.at[j, column], s_send.at[j],
+                   s_recv.at[j], (group, dp, up_t(j))).start()
+
+    def project_arrived(k, carry):
+        for q in range(chips):
+            c_arrival(k, q).wait_recv()
+        project(k)
+        return carry
+
+    own_w.wait()
+    project(0)
+    own_keys.start()
+    own_values.start()
     lax.fori_loop(1, n_tensor, spread, 0)
 
     own_down.wait()
@@ -297,6 +344,7 @@
         )
         a_copies[-1].start()
     lax.fori_loop(cut[1], cut[2], forward, 0)
+    lax.fori_loop(cut[0], cut[1], project_arrived, 0)
     for k in range(1, n_tensor):
         remote(low_all.at[from_t(k)], low_all.at[from_t(k)], a_send.at[k], a_recv.at[k],
                (group, dp, up_t(k))).wait_recv()
@@ -315,21 +363,8 @@
         r_copies[-1].start()
     corr_in[dp] = corr_out[dp]
     lax.fori_loop(cut[2], cut[3], forward, 0)
-
-    def project(k):
-        block = jnp.dot(x_ref[...], w_parts[k], preferred_element_type=jnp.float32)
-        column = from_t(k)
-        for t in range(n_tensor):
-            for s in range(steps):
-                base_out[t, column, s * row_block:(s + 1) * row_block, :] = block[
-                    s * rows + t * row_block:s * rows + (t + 1) * row_block
-                ]
-        for j in range(1, n_tensor):
-            remote(base_out.at[up_t(j), column], base_in.at[j, column], s_send.at[j],
-                   s_recv.at[j], (group, dp, up_t(j))).start()
-
-    own_w.wait()
-    project(0)
+    lax.fori_loop(cut[1], cut[2], project_arrived, 0)
+
 
     for copy in r_copies:
         copy.wait_recv()
@@ -351,13 +386,9 @@
         e_copies[-1].start()
     delta_in[tensor] = delta_out[tensor]
 
-    def project_arrived(k, carry):
-        for q in range(chips):
-            c_arrival(k, q).wait_recv()
-        project(k)
-        return carry
-
-    lax.fori_loop(1, n_tensor, project_arrived, 0)
+    lax.fori_loop(cut[2], cut[3], project_arrived, 0)
+    own_keys.wait()
+    own_values.wait()
 
     for copy in e_copies:
         copy.wait_recv()
@@ -370,7 +401,14 @@
         )
         s_waits[-1].wait_recv()
         base += base_in[j]
-    out_ref[...] = (base + delta_in[...].astype(jnp.float32)).astype(jnp.bfloat16)
+    parts = [base[t] + delta_in[t].astype(jnp.float32) for t in range(n_tensor)]
+    fresh_shape = (steps * row_block, new_keys_ref.shape[2])
+    attend(
+        steps, row_block, parts, keys_buf, values_buf,
+        new_keys_ref[...].astype(jnp.float32).reshape(fresh_shape).astype(jnp.bfloat16),
+        new_values_ref[...].astype(jnp.float32).reshape(fresh_shape).astype(jnp.bfloat16),
+        lengths_ref[...], out_ref,
+    )
 
     for copy in d_copies + l_copies + a_copies + r_copies + e_copies + s_waits:
         copy.wait_send()
@@ -416,10 +454,10 @@
     dma = pltpu.SemaphoreType.DMA
     tensor_sems = [dma((n_tensor,)), dma((n_tensor,))]
     dp_sems = [dma((n_dp,)), dma((n_dp,))]
-    queries = pl.pallas_call(
-        functools.partial(queries_kernel, sizes),
-        out_shape=jax.ShapeDtypeStruct((n_tensor, own, columns), bf16),
-        in_specs=[vmem, hbm, hbm, vmem, vmem, vmem, vmem, vmem],
+    return pl.pallas_call(
+        functools.partial(decode_kernel, sizes),
+        out_shape=jax.ShapeDtypeStruct((steps, row_block, n_tensor * columns), bf16),
+        in_specs=[vmem, hbm, hbm, vmem, vmem, vmem, hbm, hbm, vmem, vmem, vmem],
         out_specs=vmem,
         scratch_shapes=[
             pltpu.VMEM((n_tensor, depth, columns), bf16),
@@ -435,7 +473,9 @@
             pltpu.VMEM((n_tensor, own, columns), bf16),
             pltpu.VMEM((n_tensor, n_tensor, own, columns), f32),
             pltpu.VMEM((n_tensor, n_tensor, own, columns), f32),
-            dma((2,)),
+            pltpu.VMEM(cache_keys.shape, bf16),
+            pltpu.VMEM(cache_values.shape, bf16),
+            dma((4,)),
             *tensor_sems,
             *dp_sems,
             dma((n_tensor, chips)),
@@ -451,20 +491,20 @@
         compiler_params=pltpu.CompilerParams(
             collective_id=0, has_side_effects=True, vmem_limit_bytes=VMEM_BYTES
         ),
-        name="queries",
+        name="decode",
     )(
         x_feats.reshape(steps * rows, depth),
         w_query,
         jnp.swapaxes(adapter_down, 1, 2).reshape(adapters * rank, depth),
         adapter_up.reshape(adapters * rank, columns),
-        jnp.tile(agent_id, steps).reshape(1, steps * rows),
-        agent_id.reshape(rows, 1),
+        agent_id.reshape(1, rows),
         adapter_slot.reshape(1, -1),
-        adapter_slot.reshape(-1, 1),
-    )
-    row_queries = queries.reshape(n_tensor, steps, row_block, columns)
-    row_queries = row_queries.transpose(1, 2, 0, 3).reshape(steps, row_block, n_tensor * columns)
-    return attention(row_queries, cache_keys, cache_values, new_keys, new_values, lengths)
+        cache_keys,
+        cache_values,
+        new_keys,
+        new_values,
+        lengths.reshape(1, -1),
+    )
 
 
 def solution(mesh):

time: 44.1 us -> 36.3 us (0.82)
  matrix products: 3.61 us -> 0 us
  local copies, waits for them, and re-layouts: 4.65 us -> 1.38 us
  other arithmetic: 1.31 us -> 0 us
    dot_general x4 -> x0, matrix products: 3.61 us -> none  [the longest x1 1.75 us: attention(): jnp.einsum('srgqd,rjgd->srgqj', query_five, keys_four, preferred_element_...]
    reshape x2 -> x0, local copies, waits for them, and re-layouts: 2.67 us -> none  [the longest x1 1.34 us: local(): agent_id.reshape(rows, 1)]
    unnamed x8 -> x1, local copies, waits for them, and re-layouts: 0.02 us -> 1.38 us
    another operation x2 -> x0, local copies, waits for them, and re-layouts: 1.31 us -> none  [local(): jnp.tile(agent_id, steps).reshape(1, steps * rows)]
    lt x1 -> x0, other arithmetic: 0.84 us -> none  [attention(): jnp.arange(length_max)[None, :] < lengths[:, None]]
    convert_element_type x1 -> x0, local copies, waits for them, and re-layouts: 0.64 us -> none  [attention(): return mixed.astype(jnp.bfloat16).reshape(step_count, row_count, width)]
    pallas_call x1, Pallas kernels: 34.3 us -> 34.7 us  [local(): pl.pallas_call(functools.partial(decode_kernel, sizes), out_shape=jax.Sha...]
where the time goes in v2:
time: 36.3 us; the launch traced here: 36.1 us
  Pallas kernels  34.7 us (96%)
  local copies, waits for them, and re-layouts  1.38 us (4%)
    pallas_call x1, Pallas kernels, local(): pl.pallas_call(functools.partial(decode_kernel, sizes), out_shape=jax.Sha...  34.7 us
    unnamed x1, local copies, waits for them, and re-layouts  1.38 us

profile of v2, /device:TPU:0, one launch (start us, length us, event | category | flops | bytes accessed | tf_op | source)
XLA Modules:
  0.0 36.1 jit_solution(9193166297651081241)
XLA Ops:
  0.0 34.7 %decode.1 = bf16[4,8,512]{2,1,0:T(8,128)(2,1)} custom-call(bf16[128,2048]{1,0:T(8,128)(2,1)} %bitcast.9, bf16[8192,128]{1,0:T(8,128)(2,1)} %w_ref.1, bf16[512,2048]{1,0:T(8,128)(2,1)} %bitcast.8, bf16[512,128]{1,0:T(8,128)(2,1)} %bitcast.10, s32[1,32]{1,0:T(1,128)} %bitcast.11, s32[1,32]{1,0:T(1,128)} %bitcast.12, bf16[8,192,512]{2,1,0:T(8,128)(2,1)} %keys_ref.1, ...), custom_call_target="tpu_custom_call" | custom-call | tf_op jit(solution)/shard_map/decode/pallas_call | solution.py:457
  34.7 1.4 %copy.13 = bf16[4,8,512]{2,1,0:T(8,128)(2,1)} copy(bf16[4,8,512]{2,1,0:T(8,128)(2,1)} %decode.1) | data formatting | bytes 65536

commit v3 on v2

--- a/solution.py
+++ b/solution.py
@@ -11,7 +11,7 @@
 KVH = 4
 MESH = pl.DeviceIdType.MESH
 LANES = 128
-VMEM_BYTES = 60 * 1024 * 1024
+VMEM_BYTES = 62 * 1024 * 1024
 
 
 def attend(steps, row_block, parts, keys_buf, values_buf, fresh_keys, fresh_values, lengths, out_ref):
@@ -60,7 +60,6 @@
             out_ref[:, :, h * HD:(h + 1) * HD] = (
                 mixed[i * queries:(i + 1) * queries]
                 .reshape(steps, row_block, HD)
-                .astype(jnp.bfloat16)
             )
 
 
@@ -133,8 +132,12 @@
     core = lax.rem(dp, 2)
     chip = group * n_chip_x + dp // 2
 
-    def at_chip(number, which):
-        return (number // n_chip_x, lax.rem(number, n_chip_x) * 2 + which, tensor)
+    chip_x = dp // 2
+
+    def part_of(q, which):
+        g = lax.rem(group - q // n_chip_x + n_group, n_group)
+        x = lax.rem(chip_x - q % n_chip_x + n_chip_x, n_chip_x)
+        return rows_of((g * n_chip_x + x) * 2 + which, piece)
 
     sibling = (group, (dp // 2) * 2 + (1 - core), tensor)
 
@@ -169,14 +172,11 @@
     for j in range(1, n_dp):
         pl.semaphore_signal(barrier, inc=1, device_id=(group, up_d(j), tensor), device_id_type=MESH)
     for other in range(1, n_group):
-        for j in range(n_dp):
-            if j % 2 == 0:
-                pl.semaphore_signal(
-                    barrier, inc=1,
-                    device_id=(lax.rem(group + other, n_group), up_d(j), tensor),
-                    device_id_type=MESH,
-                )
-    pl.semaphore_wait(barrier, n_tensor - 1 + n_dp - 1 + (n_group - 1) * n_chip_x)
+        pl.semaphore_signal(
+            barrier, inc=1, device_id=(lax.rem(group + other, n_group), dp, tensor),
+            device_id_type=MESH,
+        )
+    pl.semaphore_wait(barrier, n_tensor - 1 + n_dp - 1 + n_group - 1)
 
     mine = rows_of(chip * 2 + core, piece)
 
@@ -248,39 +248,54 @@
     x_in[dp] = x_out[dp]
 
     def b_copy(k, q):
+        back_group, back_x = q // n_chip_x, q % n_chip_x
+        if back_group == 0:
+            part = part_of(0, core)
+            device = (group, lax.rem(chip_x + back_x, n_chip_x) * 2 + core, tensor)
+        else:
+            part = part_of(back_x, core)
+            device = (lax.rem(group + back_group, n_group), dp, tensor)
         return remote(
-            w_parts.at[k, mine], w_parts.at[k, mine], b_send.at[k, q], b_recv.at[k, q],
-            at_chip(lax.rem(chip + q, chips), core),
+            w_parts.at[k, part], w_parts.at[k, part], b_send.at[k, q], b_recv.at[k, q], device
+        )
+
+    def b_arrival(k, q):
+        part = part_of(q, core)
+        return remote(
+            w_parts.at[k, part], w_parts.at[k, part], b_send.at[k, q], b_recv.at[k, q], sibling
         )
 
     def c_copy(k, q):
-        part = rows_of(lax.rem(chip - q + chips, chips) * 2 + core, piece)
+        part = part_of(q, core)
         return remote(
             w_parts.at[k, part], w_parts.at[k, part], c_send.at[k, q], c_recv.at[k, q], sibling
         )
 
-    def b_arrival(k, q):
-        part = rows_of(lax.rem(chip - q + chips, chips) * 2 + core, piece)
-        return remote(
-            w_parts.at[k, part], w_parts.at[k, part], b_send.at[k, q], b_recv.at[k, q],
-            at_chip(lax.rem(chip + q, chips), core),
-        )
-
     def c_arrival(k, q):
-        part = rows_of(lax.rem(chip - q + chips, chips) * 2 + 1 - core, piece)
+        part = part_of(q, 1 - core)
         return remote(
             w_parts.at[k, part], w_parts.at[k, part], c_send.at[k, q], c_recv.at[k, q], sibling
         )
 
     def spread(k, carry):
         z_copy(k).wait_recv()
-        for q in range(1, chips):
-            b_copy(k, q).start()
+        for j in range(1, n_chip_x):
+            b_copy(k, j).start()
+        for other in range(1, n_group):
+            b_copy(k, other * n_chip_x).start()
         c_copy(k, 0).start()
         return carry
 
     def forward(k, carry):
-        for q in range(1, chips):
+        for j in range(1, n_chip_x):
+            b_arrival(k, j).wait_recv()
+            for other in range(1, n_group):
+                b_copy(k, other * n_chip_x + j).start()
+            c_copy(k, j).start()
+        return carry
+
+    def hand_over(k, carry):
+        for q in range(n_chip_x, chips):
             b_arrival(k, q).wait_recv()
             c_copy(k, q).start()
         return carry
@@ -344,7 +359,7 @@
         )
         a_copies[-1].start()
     lax.fori_loop(cut[1], cut[2], forward, 0)
-    lax.fori_loop(cut[0], cut[1], project_arrived, 0)
+    lax.fori_loop(cut[0], cut[1], hand_over, 0)
     for k in range(1, n_tensor):
         remote(low_all.at[from_t(k)], low_all.at[from_t(k)], a_send.at[k], a_recv.at[k],
                (group, dp, up_t(k))).wait_recv()
@@ -363,7 +378,8 @@
         r_copies[-1].start()
     corr_in[dp] = corr_out[dp]
     lax.fori_loop(cut[2], cut[3], forward, 0)
-    lax.fori_loop(cut[1], cut[2], project_arrived, 0)
+    lax.fori_loop(cut[1], cut[2], hand_over, 0)
+    lax.fori_loop(cut[0], cut[1], project_arrived, 0)
 
 
     for copy in r_copies:
@@ -386,7 +402,8 @@
         e_copies[-1].start()
     delta_in[tensor] = delta_out[tensor]
 
-    lax.fori_loop(cut[2], cut[3], project_arrived, 0)
+    lax.fori_loop(cut[2], cut[3], hand_over, 0)
+    lax.fori_loop(cut[1], cut[3], project_arrived, 0)
     own_keys.wait()
     own_values.wait()
 
@@ -456,7 +473,7 @@
     dp_sems = [dma((n_dp,)), dma((n_dp,))]
     return pl.pallas_call(
         functools.partial(decode_kernel, sizes),
-        out_shape=jax.ShapeDtypeStruct((steps, row_block, n_tensor * columns), bf16),
+        out_shape=jax.ShapeDtypeStruct((steps, row_block, n_tensor * columns), f32),
         in_specs=[vmem, hbm, hbm, vmem, vmem, vmem, hbm, hbm, vmem, vmem, vmem],
         out_specs=vmem,
         scratch_shapes=[
@@ -504,7 +521,7 @@
         new_keys,
         new_values,
         lengths.reshape(1, -1),
-    )
+    ).astype(bf16)
 
 
 def solution(mesh):

time: 36.3 us -> 37.5 us (1.033)
  other arithmetic: 0 us -> 1.46 us
  local copies, waits for them, and re-layouts: 1.38 us -> 0 us
  Pallas kernels: 34.7 us -> 35.9 us
    convert_element_type x0 -> x1, other arithmetic: none -> 1.46 us  [local(): return pl.pallas_call(functools.partial(decode_kernel, sizes), out_shape=...]
    unnamed x1 -> x0, local copies, waits for them, and re-layouts: 1.38 us -> none
    pallas_call x1, Pallas kernels: 34.7 us -> 35.9 us  [local(): pl.pallas_call(functools.partial(decode_kernel, sizes), out_shape=jax.Sha...]
where the time goes in v3:
time: 37.5 us; the launch traced here: 37.3 us
  Pallas kernels  35.9 us (96%)
  other arithmetic  1.46 us (4%)
    pallas_call x1, Pallas kernels, local(): pl.pallas_call(functools.partial(decode_kernel, sizes), out_shape=jax.Sha...  35.9 us
    convert_element_type x1, other arithmetic, local(): return pl.pallas_call(functools.partial(decode_kernel, sizes), out_shape=...  1.46 us

profile of v3, /device:TPU:0, one launch (start us, length us, event | category | flops | bytes accessed | tf_op | source)
XLA Modules:
  0.0 37.3 jit_solution(3846073865467888673)
XLA Ops:
  0.0 35.9 %decode.1 = f32[4,8,512]{2,1,0:T(8,128)} custom-call(bf16[128,2048]{1,0:T(8,128)(2,1)} %bitcast.9, bf16[8192,128]{1,0:T(8,128)(2,1)} %w_ref.1, bf16[512,2048]{1,0:T(8,128)(2,1)} %bitcast.8, bf16[512,128]{1,0:T(8,128)(2,1)} %bitcast.10, s32[1,32]{1,0:T(1,128)} %bitcast.11, s32[1,32]{1,0:T(1,128)} %bitcast.12, bf16[8,192,512]{2,1,0:T(8,128)(2,1)} %keys_ref.1, ...), custom_call_target="tpu_custom_call" | custom-call | tf_op jit(solution)/shard_map/decode/pallas_call | solution.py:474
  35.9 1.5 %convert_element_type.3 = bf16[4,8,512]{2,1,0:T(8,128)(2,1)} convert(f32[4,8,512]{2,1,0:T(8,128)} %decode.1) | non-fusion elementwise | flops 16384 | bytes 98304 | tf_op jit(solution)/shard_map/convert_element_type | solution.py:524

commit v4 on v2

--- a/solution.py
+++ b/solution.py
@@ -11,7 +11,7 @@
 KVH = 4
 MESH = pl.DeviceIdType.MESH
 LANES = 128
-VMEM_BYTES = 60 * 1024 * 1024
+VMEM_BYTES = 62 * 1024 * 1024
 
 
 def attend(steps, row_block, parts, keys_buf, values_buf, fresh_keys, fresh_values, lengths, out_ref):
@@ -343,8 +343,6 @@
                    (group, dp, up_t(k)))
         )
         a_copies[-1].start()
-    lax.fori_loop(cut[1], cut[2], forward, 0)
-    lax.fori_loop(cut[0], cut[1], project_arrived, 0)
     for k in range(1, n_tensor):
         remote(low_all.at[from_t(k)], low_all.at[from_t(k)], a_send.at[k], a_recv.at[k],
                (group, dp, up_t(k))).wait_recv()
@@ -362,8 +360,8 @@
         )
         r_copies[-1].start()
     corr_in[dp] = corr_out[dp]
-    lax.fori_loop(cut[2], cut[3], forward, 0)
-    lax.fori_loop(cut[1], cut[2], project_arrived, 0)
+    lax.fori_loop(cut[1], cut[3], forward, 0)
+    lax.fori_loop(cut[0], cut[2], project_arrived, 0)
 
 
     for copy in r_copies:

time: 36.3 us -> 36.2 us (level)
  no operation moved by 1% of the time
where the time goes in v4:
time: 36.2 us; the launch traced here: 36 us
  Pallas kernels  34.6 us (96%)
  local copies, waits for them, and re-layouts  1.38 us (4%)
    pallas_call x1, Pallas kernels, local(): pl.pallas_call(functools.partial(decode_kernel, sizes), out_shape=jax.Sha...  34.6 us
    unnamed x1, local copies, waits for them, and re-layouts  1.38 us

profile of v4, /device:TPU:0, one launch (start us, length us, event | category | flops | bytes accessed | tf_op | source)
XLA Modules:
  0.0 36.0 jit_solution(7356337563407151175)
XLA Ops:
  0.0 34.6 %decode.1 = bf16[4,8,512]{2,1,0:T(8,128)(2,1)} custom-call(bf16[128,2048]{1,0:T(8,128)(2,1)} %bitcast.9, bf16[8192,128]{1,0:T(8,128)(2,1)} %w_ref.1, bf16[512,2048]{1,0:T(8,128)(2,1)} %bitcast.8, bf16[512,128]{1,0:T(8,128)(2,1)} %bitcast.10, s32[1,32]{1,0:T(1,128)} %bitcast.11, s32[1,32]{1,0:T(1,128)} %bitcast.12, bf16[8,192,512]{2,1,0:T(8,128)(2,1)} %keys_ref.1, ...), custom_call_target="tpu_custom_call" | custom-call | tf_op jit(solution)/shard_map/decode/pallas_call | solution.py:455
  34.6 1.4 %copy.13 = bf16[4,8,512]{2,1,0:T(8,128)(2,1)} copy(bf16[4,8,512]{2,1,0:T(8,128)(2,1)} %decode.1) | data formatting | bytes 65536

commit v5 on v4

--- a/solution.py
+++ b/solution.py
@@ -308,7 +308,7 @@
     project(0)
     own_keys.start()
     own_values.start()
-    lax.fori_loop(1, n_tensor, spread, 0)
+    lax.fori_loop(cut[0], cut[2], spread, 0)
 
     own_down.wait()
     for copy in d_copies:
@@ -330,7 +330,7 @@
                    (group, dp, up_t(k)))
         )
         l_copies[-1].start()
-    lax.fori_loop(cut[0], cut[1], forward, 0)
+    lax.fori_loop(cut[2], cut[3], spread, 0)
     total = low_out[tensor]
     for k in range(1, n_tensor):
         l_copies[k - 1].wait_recv()
@@ -343,6 +343,7 @@
                    (group, dp, up_t(k)))
         )
         a_copies[-1].start()
+    lax.fori_loop(cut[0], cut[1], forward, 0)
     for k in range(1, n_tensor):
         remote(low_all.at[from_t(k)], low_all.at[from_t(k)], a_send.at[k], a_recv.at[k],
                (group, dp, up_t(k))).wait_recv()

time: 36.2 us -> 36.1 us (level)
  no operation moved by 1% of the time
where the time goes in v5:
time: 36.1 us; the launch traced here: 35.9 us
  Pallas kernels  34.5 us (96%)
  local copies, waits for them, and re-layouts  1.38 us (4%)
    pallas_call x1, Pallas kernels, local(): pl.pallas_call(functools.partial(decode_kernel, sizes), out_shape=jax.Sha...  34.5 us
    unnamed x1, local copies, waits for them, and re-layouts  1.38 us

profile of v5, /device:TPU:0, one launch (start us, length us, event | category | flops | bytes accessed | tf_op | source)
XLA Modules:
  0.0 35.9 jit_solution(16028030626103247008)
XLA Ops:
  0.0 34.5 %decode.1 = bf16[4,8,512]{2,1,0:T(8,128)(2,1)} custom-call(bf16[128,2048]{1,0:T(8,128)(2,1)} %bitcast.9, bf16[8192,128]{1,0:T(8,128)(2,1)} %w_ref.1, bf16[512,2048]{1,0:T(8,128)(2,1)} %bitcast.8, bf16[512,128]{1,0:T(8,128)(2,1)} %bitcast.10, s32[1,32]{1,0:T(1,128)} %bitcast.11, s32[1,32]{1,0:T(1,128)} %bitcast.12, bf16[8,192,512]{2,1,0:T(8,128)(2,1)} %keys_ref.1, ...), custom_call_target="tpu_custom_call" | custom-call | tf_op jit(solution)/shard_map/decode/pallas_call | solution.py:456
  34.5 1.4 %copy.13 = bf16[4,8,512]{2,1,0:T(8,128)(2,1)} copy(bf16[4,8,512]{2,1,0:T(8,128)(2,1)} %decode.1) | data formatting | bytes 65536
